TPU v7x, 128 devices: a whole 4x4x4 slice. The times are simulated.
128 devices in a mesh: comp: 2 (over z_lo), ty: 8 (over y, z_hi), tx: 8 (over x, core).
Axes of the slice: x: 4, y: 4, z: 4 (z_hi: 2, z_lo: 2; z = z_hi * 2 + z_lo), core: 2. Of those that a mesh axis runs over, the one named last changes fastest.
Arguments:
- state: float32 [2, 150, 512, 1024], P('comp', None, 'ty', 'tx'), may hold values from -6 to 6
- diffusivity: float32 [2, 150], P('comp'), may hold values from 0.02 to 0.2
- mixing: float32 [2, 150, 150], P('comp'), may hold values from -0.5 to 0.5
- ocean_mask: int32 [512, 1024], P('ty', 'tx'), may hold values 0 or 1
- flux_dest: int32 [8, 512, 1], P('tx', 'ty'), may hold values from 0 to 63; in each aligned block of 64 rows (0 to 63, 64 to 127, ..., all dimensions but the last counted through in order) at most 2 rows name the same one
- flux_target: int32 [8, 512], P('tx', 'ty'), may hold values from 0 to 63
- flux_weight: float32 [8, 512], P('tx', 'ty'), may hold values from 0.5 to 1.5
- fold_source: int32 [1024], P('tx'), may hold values from 0 to 1023, each once
Outputs:
- final_state: float32 [2, 150, 512, 1024], P('comp', None, 'ty', 'tx')
Inputs may be any that keep to these rules, and one draw needn't show every extreme that they name: `flux_dest`: among the 64 rows of one device (aligned blocks of 64 rows in the flattened order) no ocean tile is named more than 2 times. `fold_source`: A permutation of the 1024 columns.
All inputs are finite; a program needn't handle non-finite values. No bound on the sum of `ocean_mask` on one device may be relied on, other than what follows from the above.
Results may differ from a plain program's by a relative error of at most 0.0001.
Values sent between devices are 32-bit elements; how exact they have to be, the bound alone decides.
No kernel may reach another device: no remote copies, remote signals or barrier semaphores. Data moves between devices by JAX's collectives and lax.ppermute only.
A program may use at most 192 MiB of HBM per device.

v0:
```python
import jax
import jax.numpy as jnp
from jax import lax
from jax.sharding import PartitionSpec as P

NSTEP = 4
INTERVALS = 2


relaxation_speed = 0.3
flux_gain = 0.25
mix_gain = 0.1


def with_halo(cells, sides, width, closed):
    for axis, dim in sides:
        count = lax.axis_size(axis)
        ends = count if closed else count - 1
        head = lax.slice_in_dim(cells, 0, width, axis=dim)
        tail = lax.slice_in_dim(cells, cells.shape[dim] - width, cells.shape[dim], axis=dim)
        cells = jnp.concatenate(
            [
                lax.ppermute(tail, axis, [(i, (i + 1) % count) for i in range(ends)]),
                cells,
                lax.ppermute(head, axis, [((i + 1) % count, i) for i in range(ends)]),
            ],
            axis=dim,
        )
    return cells


def pull_uppermost_layer(current_ocean_snapshot, vertical_layer_total):
    return jnp.stack([current_ocean_snapshot[0], current_ocean_snapshot[vertical_layer_total]])


def per_device(
    state, diffusivity, mixing, ocean_mask, flux_dest, flux_target, flux_weight, fold_source
):
    current_ocean_snapshot = state[0]
    diffuse = diffusivity[0]
    blend_mat = mixing[0]
    channels, row_count, col_count = current_ocean_snapshot.shape
    vertical_layer_total = channels // 2
    is_ocean = lax.axis_index("comp") == 1
    northmost = lax.axis_index("ty") == lax.axis_size("ty") - 1
    tile_count = lax.axis_size("ty") * lax.axis_size("tx")
    slot_count = max(2, 2 * row_count // tile_count)
    air_side = jnp.where(is_ocean, 0.0, 1.0).astype(jnp.float32)
    sea_mask = jnp.where(is_ocean, ocean_mask.astype(jnp.float32), 1.0)
    dest_tile = flux_dest[0, :, 0]
    target = flux_target[0]
    weight = flux_weight[0]
    tile_hit = (dest_tile[:, None] == jnp.arange(tile_count, dtype=jnp.int32)[None, :]).astype(
        jnp.int32
    )
    slot_rank = jnp.sum(tile_hit * (jnp.cumsum(tile_hit, axis=0) - 1), axis=1)
    picker = (dest_tile * slot_count + slot_rank)[None, :] == jnp.arange(
        tile_count * slot_count, dtype=jnp.int32
    )[:, None]
    pick_mat = picker.astype(jnp.float32)
    out_ids = jnp.sum(jnp.where(picker, target[None, :] + 1, 0), axis=1) - 1
    out_ids = jnp.where(is_ocean, -1, out_ids).reshape(tile_count, slot_count)
    high = lax.Precision.HIGHEST
    col_index = lax.broadcasted_iota(jnp.int32, (1, 1, col_count), 2)
    row_index = lax.broadcasted_iota(jnp.int32, (1, row_count, 1), 1)
    for interval in range(INTERVALS):
        surface = pull_uppermost_layer(current_ocean_snapshot, vertical_layer_total)
        outgoing = (
            jnp.einsum("kj,fjx->kfx", pick_mat, surface * weight[None, :, None], precision=high)
            * air_side
        )
        outgoing = outgoing.reshape(tile_count, slot_count, 2, col_count)
        outbound = jnp.concatenate([jnp.zeros_like(outgoing), outgoing], axis=0)
        outbound_ids = jnp.concatenate([jnp.full_like(out_ids, -1), out_ids], axis=0)
        arrived, arrived_ids = (
            lax.all_to_all(outbound, ("comp", "ty", "tx"), split_axis=0, concat_axis=0, tiled=True),
            lax.all_to_all(
                outbound_ids, ("comp", "ty", "tx"), split_axis=0, concat_axis=0, tiled=True
            ),
        )
        arrived = arrived[:tile_count]
        arrived_ids = arrived_ids[:tile_count]
        place_mat = (
            arrived_ids.reshape(-1)[None, :] == jnp.arange(row_count, dtype=jnp.int32)[:, None]
        ).astype(jnp.float32)
        flux_here = jnp.einsum(
            "yk,kfx->fyx", place_mat, arrived.reshape(-1, 2, col_count), precision=high
        )
        reply_rows = jnp.einsum("yk,fyx->kfx", place_mat, surface, precision=high).reshape(
            tile_count, slot_count, 2, col_count
        )
        outbound_back = jnp.concatenate([reply_rows, jnp.zeros_like(reply_rows)], axis=0)
        returned = lax.all_to_all(
            outbound_back, ("comp", "ty", "tx"), split_axis=0, concat_axis=0, tiled=True
        )[tile_count:]
        tile_sea_skin_heat = jnp.einsum(
            "kj,kfx->fjx", pick_mat, returned.reshape(-1, 2, col_count), precision=high
        )
        for substep in range(NSTEP):
            forcing = jnp.where(
                is_ocean,
                flux_gain * flux_here,
                relaxation_speed
                * (
                    tile_sea_skin_heat
                    - pull_uppermost_layer(current_ocean_snapshot, vertical_layer_total)
                ),
            )
            lon_edges = jnp.stack(
                [current_ocean_snapshot[:, :, 0], current_ocean_snapshot[:, :, col_count - 1]],
                axis=2,
            )
            lon_padded = with_halo(lon_edges, (("tx", 2),), 1, True)
            lat_edges = jnp.stack(
                [current_ocean_snapshot[:, 0, :], current_ocean_snapshot[:, row_count - 1, :]],
                axis=1,
            )
            lat_padded = with_halo(lat_edges, (("ty", 1),), 1, False)
            top_rows = lax.all_gather(
                current_ocean_snapshot[:, row_count - 1, :], "tx", axis=1, tiled=True
            )
            folded = jnp.take(top_rows, fold_source, axis=1)
            upper_row = jnp.where(jnp.logical_and(is_ocean, northmost), folded, lat_padded[:, 3, :])
            east_cells = jnp.where(
                col_index == col_count - 1,
                lon_padded[:, :, 3][:, :, None],
                jnp.roll(current_ocean_snapshot, -1, axis=2),
            )
            west_cells = jnp.where(
                col_index == 0,
                lon_padded[:, :, 0][:, :, None],
                jnp.roll(current_ocean_snapshot, 1, axis=2),
            )
            north_cells = jnp.where(
                row_index == row_count - 1,
                upper_row[:, None, :],
                jnp.roll(current_ocean_snapshot, -1, axis=1),
            )
            south_cells = jnp.where(
                row_index == 0,
                lat_padded[:, 0, :][:, None, :],
                jnp.roll(current_ocean_snapshot, 1, axis=1),
            )
            laplace = (
                east_cells + west_cells + north_cells + south_cells - 4.0 * current_ocean_snapshot
            )
            tendency = diffuse[:, None, None] * laplace
            tendency = tendency + mix_gain * jnp.einsum(
                "ab,byx->ayx", blend_mat, current_ocean_snapshot, precision=high
            )
            tendency = tendency.at[0].add(forcing[0]).at[vertical_layer_total].add(forcing[1])
            current_ocean_snapshot = current_ocean_snapshot + tendency * sea_mask
    return current_ocean_snapshot[None]


def solution(mesh):
    in_specs = (
        P("comp", None, "ty", "tx"),
        P("comp", None),
        P("comp", None, None),
        P("ty", "tx"),
        P("tx", "ty", None),
        P("tx", "ty"),
        P("tx", "ty"),
        P("tx"),
    )
    out_specs = P("comp", None, "ty", "tx")
    return jax.shard_map(
        per_device, mesh=mesh, in_specs=in_specs, out_specs=out_specs, check_vma=False
    )
```

profile of v0, /device:TPU:9, one launch (start us, length us, event | category | flops | bytes accessed | tf_op | source)
XLA Modules:
  0.0 782.5 jit_solution(11715976023567862558)
XLA Ops:
  29.7 11.1 %all-to-all-start.1 = ((s32[128,1,2]{2,1,0:T(1,128)}), s32[128,1,2]{2,1,0:T(1,128)S(1)}, u32[]{:S(2)}, u32[]{:S(2)}) async-start(s32[128,1,2]{2,1,0:T(1,128)} %bitcast.17), calls=%async_computation.1 | async-start | bytes 131072 | tf_op jit(solution)/shard_map/all_to_all | solution.py:77
  40.8 13.7 %all-gather = f32[150,1,1024]{2,0,1:T(8,128)S(1)} all-gather(f32[150,1,128]{2,0,1:T(8,128)S(1)} %get-tuple-element.238), channel_id=2, replica_groups=mesh['comp'=2,'ty'=8,'tx'=8] {'tx'}, dimensions={2}, use_global_device_ids=true | all-gather | bytes 691200 | tf_op jit(solution)/shard_map/all_gather | solution.py:119
  54.5 9.1 %fusion.141 = (f32[150,64,127]{2,0,1:T(8,128)}, f32[150,64,127]{2,0,1:T(8,128)}) fusion(f32[150,64,128]{2,0,1:T(8,128)} %bitcast.186), kind=kLoop, calls=%fused_computation.248 | loop fusion | bytes 19507200 | tf_op jit(solution)/shard_map/jit(_roll_static)/slice | solution.py:132
  71.6 9.0 %all-to-all-start = ((f32[128,2,2,128]{3,1,2,0:T(2,128)}), f32[128,2,2,128]{3,1,2,0:T(2,128)S(1)}, u32[]{:S(2)}, u32[]{:S(2)}) async-start(f32[128,2,2,128]{3,1,2,0:T(2,128)} %concatenate.152), calls=%async_computation | async-start | bytes 524288 | tf_op jit(solution)/shard_map/all_to_all | solution.py:76
  96.1 18.4 %fusion.5 = f32[150,64,128]{2,0,1:T(8,128)} fusion(f32[150,64,1]{2,0,1:T(8,128)} %get-tuple-element.243, f32[150,64,127]{2,0,1:T(8,128)} %get-tuple-element.245, f32[150,64,127]{2,0,1:T(8,128)} %get-tuple-element.244, f32[150,64,1]{2,0,1:T(8,128)} %get-tuple-element.242, f32[150,1,128]{2,0,1:T(8,128)S(1)} %get-tuple-element.239, ...), kind=kOutput, calls=%fused_computation.14 | convolution fusion | flops 2231500800 | bytes 29812584 | tf_op jit(solution)/shard_map/ab,byx->ayx/dot_general | solution.py:148
  143.0 13.7 %all-gather.1 = f32[150,1,1024]{2,0,1:T(8,128)S(1)} all-gather(f32[150,1,128]{2,0,1:T(8,128)S(1)} %get-tuple-element.230), channel_id=3, replica_groups=mesh['comp'=2,'ty'=8,'tx'=8] {'tx'}, dimensions={2}, use_global_device_ids=true | all-gather | bytes 691200 | tf_op jit(solution)/shard_map/all_gather | solution.py:119
  176.3 19.0 %fusion.11 = f32[150,64,128]{2,0,1:T(8,128)S(1)} fusion(f32[150,64,1]{2,0,1:T(8,128)} %get-tuple-element.235, f32[150,64,127]{2,0,1:T(8,128)} %get-tuple-element.237, f32[150,64,127]{2,0,1:T(8,128)} %get-tuple-element.236, f32[150,64,1]{2,0,1:T(8,128)} %get-tuple-element.234, f32[150,1,128]{2,0,1:T(8,128)S(1)} %get-tuple-element.231, ...), kind=kOutput, calls=%fused_computation.24 | convolution fusion | flops 2231500800 | bytes 29812584 | tf_op jit(solution)/shard_map/ab,byx->ayx/dot_general | solution.py:148
  221.9 17.2 %all-gather.2 = f32[150,1,1024]{2,0,1:T(8,128)S(1)} all-gather(f32[150,1,128]{2,0,1:T(8,128)S(1)} %get-tuple-element.220), channel_id=4, replica_groups=mesh['comp'=2,'ty'=8,'tx'=8] {'tx'}, dimensions={2}, use_global_device_ids=true | all-gather | bytes 691200 | tf_op jit(solution)/shard_map/all_gather | solution.py:119
  258.3 19.0 %fusion.17 = f32[150,64,128]{2,0,1:T(8,128)S(1)} fusion(f32[150,64,1]{2,0,1:T(8,128)} %get-tuple-element.225, f32[150,64,127]{2,0,1:T(8,128)} %get-tuple-element.227, f32[150,64,127]{2,0,1:T(8,128)} %get-tuple-element.226, f32[150,64,1]{2,0,1:T(8,128)} %get-tuple-element.224, f32[150,1,128]{2,0,1:T(8,128)S(1)} %get-tuple-element.221, ...), kind=kOutput, calls=%fused_computation.34 | convolution fusion | flops 2231500800 | bytes 29812584 | tf_op jit(solution)/shard_map/ab,byx->ayx/dot_general | solution.py:148
  304.0 15.5 %all-gather.3 = f32[150,1,1024]{2,0,1:T(8,128)S(1)} all-gather(f32[150,1,128]{2,0,1:T(8,128)S(1)} %get-tuple-element.210), channel_id=5, replica_groups=mesh['comp'=2,'ty'=8,'tx'=8] {'tx'}, dimensions={2}, use_global_device_ids=true | all-gather | bytes 691200 | tf_op jit(solution)/shard_map/all_gather | solution.py:119
  338.8 19.0 %fusion.23 = f32[150,64,128]{2,0,1:T(8,128)S(1)} fusion(f32[150,64,1]{2,0,1:T(8,128)} %get-tuple-element.215, f32[150,64,127]{2,0,1:T(8,128)} %get-tuple-element.217, f32[150,64,127]{2,0,1:T(8,128)} %get-tuple-element.216, f32[150,64,1]{2,0,1:T(8,128)} %get-tuple-element.214, f32[150,1,128]{2,0,1:T(8,128)S(1)} %get-tuple-element.211, ...), kind=kOutput, calls=%fused_computation.44 | convolution fusion | flops 2231500800 | bytes 29812584 | tf_op jit(solution)/shard_map/ab,byx->ayx/dot_general | solution.py:148
  393.3 14.2 %all-gather.4 = f32[150,1,1024]{2,0,1:T(8,128)S(1)} all-gather(f32[150,1,128]{2,0,1:T(8,128)S(1)} %get-tuple-element.200), channel_id=6, replica_groups=mesh['comp'=2,'ty'=8,'tx'=8] {'tx'}, dimensions={2}, use_global_device_ids=true | all-gather | bytes 691200 | tf_op jit(solution)/shard_map/all_gather | solution.py:119
  427.4 10.3 %all-to-all-start.4 = ((f32[128,2,2,128]{3,1,2,0:T(2,128)}), f32[128,2,2,128]{3,1,2,0:T(2,128)S(1)}, u32[]{:S(2)}, u32[]{:S(2)}) async-start(f32[128,2,2,128]{3,1,2,0:T(2,128)} %concatenate.172), calls=%async_computation.4 | async-start | bytes 524288 | tf_op jit(solution)/shard_map/all_to_all | solution.py:93
  437.7 19.0 %fusion.29 = f32[150,64,128]{2,0,1:T(8,128)S(1)} fusion(f32[150,64,1]{2,0,1:T(8,128)} %get-tuple-element.205, f32[150,64,127]{2,0,1:T(8,128)} %get-tuple-element.207, f32[150,64,127]{2,0,1:T(8,128)} %get-tuple-element.206, f32[150,64,1]{2,0,1:T(8,128)} %get-tuple-element.204, f32[150,1,128]{2,0,1:T(8,128)S(1)} %get-tuple-element.201, ...), kind=kOutput, calls=%fused_computation.54 | convolution fusion | flops 2231500800 | bytes 29812584 | tf_op jit(solution)/shard_map/ab,byx->ayx/dot_general | solution.py:148
  484.0 13.7 %all-gather.5 = f32[150,1,1024]{2,0,1:T(8,128)S(1)} all-gather(f32[150,1,128]{2,0,1:T(8,128)S(1)} %copy.326), channel_id=7, replica_groups=mesh['comp'=2,'ty'=8,'tx'=8] {'tx'}, dimensions={2}, use_global_device_ids=true | all-gather | bytes 691200 | tf_op jit(solution)/shard_map/all_gather | solution.py:119
  502.9 10.6 %fusion.51 = f32[64,128,150]{1,2,0:T(8,128)} fusion(f32[1,150,150]{2,0,1:T(1,128)S(1)} %copy-done.13, f32[150,64,128]{2,1,0:T(8,128)S(1)} %copy_add_fusion), kind=kOutput, calls=%fused_computation.110 | convolution fusion | flops 2211840000 | bytes 9920400 | tf_op jit(solution)/shard_map/ab,byx->ayx/dot_general | solution.py:148
  561.5 8.3 %fusion.32 = f32[150,64,128]{2,0,1:T(8,128)} fusion(f32[150,64,1]{2,0,1:T(8,128)S(1)} %bitcast.191, f32[150,64,127]{2,0,1:T(8,128)S(1)} %copy.320, f32[150,64,127]{2,0,1:T(8,128)S(1)} %copy.321, f32[150,64,1]{2,0,1:T(8,128)S(1)} %bitcast.197, f32[150,1,128]{2,0,1:T(8,128)S(1)} %copy.323, f32[150,63,128]{2,0,1:T(8,128)S(1)} %copy-done.12, ...), kind=kLoop, calls=%fused_computation.61 | loop fusion | flops 13516800 | bytes 24806784 | tf_op jit(solution)/shard_map/add | solution.py:145
  592.2 10.7 %fusion.49 = f32[64,128,150]{1,2,0:T(8,128)} fusion(f32[1,150,150]{2,0,1:T(1,128)S(1)} %copy-done.13, f32[150,64,128]{2,1,0:T(8,128)S(1)} %multiply_add_fusion.5), kind=kOutput, calls=%fused_computation.108 | convolution fusion | flops 2211840000 | bytes 9920400 | tf_op jit(solution)/shard_map/ab,byx->ayx/dot_general | solution.py:148
  602.9 11.7 %all-gather.6 = f32[150,1,1024]{2,1,0:T(1,128)S(1)} all-gather(f32[150,1,128]{2,1,0:T(1,128)S(1)} %get-tuple-element.261), channel_id=8, replica_groups=mesh['comp'=2,'ty'=8,'tx'=8] {'tx'}, dimensions={2}, use_global_device_ids=true | all-gather | bytes 691200 | tf_op jit(solution)/shard_map/all_gather | solution.py:119
  662.5 8.3 %fusion.34 = f32[150,64,128]{2,0,1:T(8,128)S(1)} fusion(f32[150,64,1]{2,0,1:T(8,128)S(1)} %bitcast.193, f32[150,64,127]{2,0,1:T(8,128)S(1)} %copy.328, f32[150,64,127]{2,0,1:T(8,128)S(1)} %copy.329, f32[150,64,1]{2,0,1:T(8,128)S(1)} %bitcast.199, f32[150,1,128]{2,0,1:T(8,128)S(1)} %copy.331, f32[150,63,128]{2,0,1:T(8,128)} %copy.332, ...), kind=kLoop, calls=%fused_computation.67 | loop fusion | flops 9830400 | bytes 19814720 | tf_op jit(solution)/shard_map/add | solution.py:145
  670.8 8.9 %fusion.39 = f32[150,64,128]{2,1,0:T(8,128)S(1)} fusion(f32[150,63,128]{2,1,0:T(8,128)} %get-tuple-element.259, f32[150,1,128]{2,1,0:T(1,128)S(1)} %get-tuple-element.261, f32[64,128,150]{1,2,0:T(8,128)} %fusion.49, f32[150,64,128]{2,0,1:T(8,128)S(1)} %fusion.34, f32[150,64,128]{2,1,0:T(8,128)S(1)} %bitcast.183, f32[150,128]{1,0:T(8,128)S(1)} %bitcast.228, ...), kind=kLoop, calls=%fused_computation.82 | loop fusion | flops 9830400 | bytes 24653464 | tf_op jit(solution)/shard_map/add | solution.py:148
  695.8 10.7 %fusion.47 = f32[64,128,150]{1,2,0:T(8,128)} fusion(f32[1,150,150]{2,0,1:T(1,128)S(1)} %copy-done.13, f32[150,64,128]{2,1,0:T(8,128)S(1)} %multiply_add_fusion.4), kind=kOutput, calls=%fused_computation.106 | convolution fusion | flops 2211840000 | bytes 9920400 | tf_op jit(solution)/shard_map/ab,byx->ayx/dot_general | solution.py:148
  706.5 10.6 %all-gather.7 = f32[150,1,1024]{2,1,0:T(1,128)S(1)} all-gather(f32[150,1,128]{2,1,0:T(1,128)S(1)} %get-tuple-element.252), channel_id=9, replica_groups=mesh['comp'=2,'ty'=8,'tx'=8] {'tx'}, dimensions={2}, use_global_device_ids=true | all-gather | bytes 691200 | tf_op jit(solution)/shard_map/all_gather | solution.py:119
  768.1 10.5 %fusion.44 = f32[150,64,128]{2,1,0:T(8,128)S(1)} fusion(f32[150,1,128]{2,1,0:T(1,128)S(1)} %get-tuple-element.253, f32[150,63,128]{2,1,0:T(8,128)} %get-tuple-element.255, f32[150,63,128]{2,1,0:T(8,128)} %get-tuple-element.254, f32[150,1,128]{2,1,0:T(1,128)S(1)} %get-tuple-element.252, f32[64,128,150]{1,2,0:T(8,128)} %fusion.47, ...), kind=kLoop, calls=%fused_computation.88 | loop fusion | flops 13516800 | bytes 29645528 | tf_op jit(solution)/shard_map/add | solution.py:148
  (365 shorter events, 468.2 us)
Async XLA Ops:
  5.3 76.7 %collective-permute-start.2 = (f32[150,1,128]{2,0,1:T(8,128)S(1)}, f32[150,1,128]{2,0,1:T(8,128)S(1)}, u32[]{:S(2)}, u32[]{:S(2)}) collective-permute-start(f32[150,1,128]{2,0,1:T(8,128)S(1)} %get-tuple-element.239), channel_id=1, source_target_pairs={{8,0},{16,8},{24,16},{32,24},{40,32},{48,40},{56,48},{9,1},{17,9},... | collective-permute-start | bytes 230408 | tf_op jit(solution)/shard_map/ppermute | solution.py:25
  10.7 85.4 %collective-permute-start.3 = (f32[150,1,128]{2,0,1:T(8,128)S(1)}, f32[150,1,128]{2,0,1:T(8,128)S(1)}, u32[]{:S(2)}, u32[]{:S(2)}) collective-permute-start(f32[150,1,128]{2,0,1:T(8,128)S(1)} %get-tuple-element.238), channel_id=1, source_target_pairs={{0,8},{8,16},{16,24},{24,32},{32,40},{40,48},{48,56},{1,9},{9,17},... | collective-permute-start | bytes 230408 | tf_op jit(solution)/shard_map/ppermute | solution.py:23
  22.2 73.9 %collective-permute-start = (f32[150,64,1]{0,1,2:T(8,128)S(1)}, f32[150,64,1]{0,1,2:T(8,128)S(1)}, u32[]{:S(2)}, u32[]{:S(2)}) collective-permute-start(f32[150,64,1]{0,1,2:T(8,128)S(1)} %copy.113), channel_id=1, source_target_pairs={{1,0},{2,1},{3,2},{4,3},{5,4},{6,5},{7,6},{0,7},{9,8},{10,9},{11,1... | collective-permute-start | bytes 115208 | tf_op jit(solution)/shard_map/ppermute | solution.py:25
  27.3 68.8 %collective-permute-start.1 = (f32[150,64,1]{0,1,2:T(8,128)S(1)}, f32[150,64,1]{0,1,2:T(8,128)S(1)}, u32[]{:S(2)}, u32[]{:S(2)}) collective-permute-start(f32[150,64,1]{0,1,2:T(8,128)S(1)} %copy.114), channel_id=1, source_target_pairs={{0,1},{1,2},{2,3},{3,4},{4,5},{5,6},{6,7},{7,0},{8,9},{9,10},{10,1... | collective-permute-start | bytes 115208 | tf_op jit(solution)/shard_map/ppermute | solution.py:23
  29.7 41.9 %all-to-all-start.1 = ((s32[128,1,2]{2,1,0:T(1,128)}), s32[128,1,2]{2,1,0:T(1,128)S(1)}, u32[]{:S(2)}, u32[]{:S(2)}) async-start(s32[128,1,2]{2,1,0:T(1,128)} %bitcast.17), calls=%async_computation.1 | async-start | bytes 131072 | tf_op jit(solution)/shard_map/all_to_all | solution.py:77
  71.6 18.2 %all-to-all-start = ((f32[128,2,2,128]{3,1,2,0:T(2,128)}), f32[128,2,2,128]{3,1,2,0:T(2,128)S(1)}, u32[]{:S(2)}, u32[]{:S(2)}) async-start(f32[128,2,2,128]{3,1,2,0:T(2,128)} %concatenate.152), calls=%async_computation | async-start | bytes 524288 | tf_op jit(solution)/shard_map/all_to_all | solution.py:76
  89.8 25.0 %all-to-all-start.2 = ((f32[128,2,2,128]{3,1,2,0:T(2,128)}), f32[128,2,2,128]{3,1,2,0:T(2,128)S(1)}, u32[]{:S(2)}, u32[]{:S(2)}) async-start(f32[128,2,2,128]{3,1,2,0:T(2,128)} %concatenate.154), calls=%async_computation.2 | async-start | bytes 524288 | tf_op jit(solution)/shard_map/all_to_all | solution.py:93
  156.7 19.6 %collective-permute-start.7 = (f32[150,1,128]{2,0,1:T(8,128)S(1)}, f32[150,1,128]{2,0,1:T(8,128)S(1)}, u32[]{:S(2)}, u32[]{:S(2)}) collective-permute-start(f32[150,1,128]{2,0,1:T(8,128)S(1)} %get-tuple-element.230), channel_id=1, source_target_pairs={{0,8},{8,16},{16,24},{24,32},{32,40},{40,48},{48,56},{1,9},{9,17},... | collective-permute-start | bytes 230408 | tf_op jit(solution)/shard_map/ppermute | solution.py:23
  239.1 19.2 %collective-permute-start.11 = (f32[150,1,128]{2,0,1:T(8,128)S(1)}, f32[150,1,128]{2,0,1:T(8,128)S(1)}, u32[]{:S(2)}, u32[]{:S(2)}) collective-permute-start(f32[150,1,128]{2,0,1:T(8,128)S(1)} %get-tuple-element.220), channel_id=1, source_target_pairs={{0,8},{8,16},{16,24},{24,32},{32,40},{40,48},{48,56},{1,9},{9,17},... | collective-permute-start | bytes 230408 | tf_op jit(solution)/shard_map/ppermute | solution.py:23
  319.5 19.3 %collective-permute-start.15 = (f32[150,1,128]{2,0,1:T(8,128)S(1)}, f32[150,1,128]{2,0,1:T(8,128)S(1)}, u32[]{:S(2)}, u32[]{:S(2)}) collective-permute-start(f32[150,1,128]{2,0,1:T(8,128)S(1)} %get-tuple-element.210), channel_id=1, source_target_pairs={{0,8},{8,16},{16,24},{24,32},{32,40},{40,48},{48,56},{1,9},{9,17},... | collective-permute-start | bytes 230408 | tf_op jit(solution)/shard_map/ppermute | solution.py:23
  385.6 41.8 %all-to-all-start.3 = ((f32[128,2,2,128]{3,1,2,0:T(2,128)}), f32[128,2,2,128]{3,1,2,0:T(2,128)S(1)}, u32[]{:S(2)}, u32[]{:S(2)}) async-start(f32[128,2,2,128]{3,1,2,0:T(2,128)} %concatenate.171), calls=%async_computation.3 | async-start | bytes 524288 | tf_op jit(solution)/shard_map/all_to_all | solution.py:76
  407.6 19.8 %collective-permute-start.18 = (f32[150,1,128]{2,0,1:T(8,128)S(1)}, f32[150,1,128]{2,0,1:T(8,128)S(1)}, u32[]{:S(2)}, u32[]{:S(2)}) collective-permute-start(f32[150,1,128]{2,0,1:T(8,128)S(1)} %get-tuple-element.201), channel_id=1, source_target_pairs={{8,0},{16,8},{24,16},{32,24},{40,32},{48,40},{56,48},{9,1},{17,9},... | collective-permute-start | bytes 230408 | tf_op jit(solution)/shard_map/ppermute | solution.py:25
  412.9 24.8 %collective-permute-start.19 = (f32[150,1,128]{2,0,1:T(8,128)S(1)}, f32[150,1,128]{2,0,1:T(8,128)S(1)}, u32[]{:S(2)}, u32[]{:S(2)}) collective-permute-start(f32[150,1,128]{2,0,1:T(8,128)S(1)} %get-tuple-element.200), channel_id=1, source_target_pairs={{0,8},{8,16},{16,24},{24,32},{32,40},{40,48},{48,56},{1,9},{9,17},... | collective-permute-start | bytes 230408 | tf_op jit(solution)/shard_map/ppermute | solution.py:23
  427.4 33.1 %all-to-all-start.4 = ((f32[128,2,2,128]{3,1,2,0:T(2,128)}), f32[128,2,2,128]{3,1,2,0:T(2,128)S(1)}, u32[]{:S(2)}, u32[]{:S(2)}) async-start(f32[128,2,2,128]{3,1,2,0:T(2,128)} %concatenate.172), calls=%async_computation.4 | async-start | bytes 524288 | tf_op jit(solution)/shard_map/all_to_all | solution.py:93
  497.7 63.8 %collective-permute-start.23 = (f32[150,1,128]{2,0,1:T(8,128)S(1)}, f32[150,1,128]{2,0,1:T(8,128)S(1)}, u32[]{:S(2)}, u32[]{:S(2)}) collective-permute-start(f32[150,1,128]{2,0,1:T(8,128)S(1)} %copy.326), channel_id=1, source_target_pairs={{0,8},{8,16},{16,24},{24,32},{32,40},{40,48},{48,56},{1,9},{9,17},... | collective-permute-start | bytes 230408 | tf_op jit(solution)/shard_map/ppermute | solution.py:23
  513.5 47.9 %collective-permute-start.22 = (f32[150,1,128]{2,0,1:T(8,128)S(1)}, f32[150,1,128]{2,0,1:T(8,128)S(1)}, u32[]{:S(2)}, u32[]{:S(2)}) collective-permute-start(f32[150,1,128]{2,0,1:T(8,128)S(1)} %copy.323), channel_id=1, source_target_pairs={{8,0},{16,8},{24,16},{32,24},{40,32},{48,40},{56,48},{9,1},{17,9},... | collective-permute-start | bytes 230408 | tf_op jit(solution)/shard_map/ppermute | solution.py:25
  525.3 36.2 %collective-permute-start.20 = (f32[150,64,1]{0,1,2:T(8,128)S(1)}, f32[150,64,1]{0,1,2:T(8,128)S(1)}, u32[]{:S(2)}, u32[]{:S(2)}) collective-permute-start(f32[150,64,1]{0,1,2:T(8,128)S(1)} %copy.183), channel_id=1, source_target_pairs={{1,0},{2,1},{3,2},{4,3},{5,4},{6,5},{7,6},{0,7},{9,8},{10,9},{11,1... | collective-permute-start | bytes 115208 | tf_op jit(solution)/shard_map/ppermute | solution.py:25
  539.0 22.4 %collective-permute-start.21 = (f32[150,64,1]{0,1,2:T(8,128)S(1)}, f32[150,64,1]{0,1,2:T(8,128)S(1)}, u32[]{:S(2)}, u32[]{:S(2)}) collective-permute-start(f32[150,64,1]{0,1,2:T(8,128)S(1)} %copy.186), channel_id=1, source_target_pairs={{0,1},{1,2},{2,3},{3,4},{4,5},{5,6},{6,7},{7,0},{8,9},{9,10},{10,1... | collective-permute-start | bytes 115208 | tf_op jit(solution)/shard_map/ppermute | solution.py:23
  614.6 56.1 %collective-permute-start.27 = (f32[150,1,128]{2,1,0:T(1,128)S(1)}, f32[150,1,128]{2,1,0:T(1,128)S(1)}, u32[]{:S(2)}, u32[]{:S(2)}) collective-permute-start(f32[150,1,128]{2,1,0:T(1,128)S(1)} %get-tuple-element.261), channel_id=1, source_target_pairs={{0,8},{8,16},{16,24},{24,32},{32,40},{40,48},{48,56},{1,9},{9,17},... | collective-permute-start | bytes 230408 | tf_op jit(solution)/shard_map/ppermute | solution.py:23
  618.8 43.5 %collective-permute-start.26 = (f32[150,1,128]{2,0,1:T(8,128)S(1)}, f32[150,1,128]{2,0,1:T(8,128)S(1)}, u32[]{:S(2)}, u32[]{:S(2)}) collective-permute-start(f32[150,1,128]{2,0,1:T(8,128)S(1)} %copy.331), channel_id=1, source_target_pairs={{8,0},{16,8},{24,16},{32,24},{40,32},{48,40},{56,48},{9,1},{17,9},... | collective-permute-start | bytes 230408 | tf_op jit(solution)/shard_map/ppermute | solution.py:25
  631.5 30.9 %collective-permute-start.24 = (f32[150,64,1]{0,1,2:T(8,128)S(1)}, f32[150,64,1]{0,1,2:T(8,128)S(1)}, u32[]{:S(2)}, u32[]{:S(2)}) collective-permute-start(f32[150,64,1]{0,1,2:T(8,128)S(1)} %copy.200), channel_id=1, source_target_pairs={{1,0},{2,1},{3,2},{4,3},{5,4},{6,5},{7,6},{0,7},{9,8},{10,9},{11,1... | collective-permute-start | bytes 115208 | tf_op jit(solution)/shard_map/ppermute | solution.py:25
  717.1 50.9 %collective-permute-start.31 = (f32[150,1,128]{2,1,0:T(1,128)S(1)}, f32[150,1,128]{2,1,0:T(1,128)S(1)}, u32[]{:S(2)}, u32[]{:S(2)}) collective-permute-start(f32[150,1,128]{2,1,0:T(1,128)S(1)} %get-tuple-element.252), channel_id=1, source_target_pairs={{0,8},{8,16},{16,24},{24,32},{32,40},{40,48},{48,56},{1,9},{9,17},... | collective-permute-start | bytes 230408 | tf_op jit(solution)/shard_map/ppermute | solution.py:23
  720.4 47.6 %collective-permute-start.30 = (f32[150,1,128]{2,1,0:T(1,128)S(1)}, f32[150,1,128]{2,1,0:T(1,128)S(1)}, u32[]{:S(2)}, u32[]{:S(2)}) collective-permute-start(f32[150,1,128]{2,1,0:T(1,128)S(1)} %get-tuple-element.253), channel_id=1, source_target_pairs={{8,0},{16,8},{24,16},{32,24},{40,32},{48,40},{56,48},{9,1},{17,9},... | collective-permute-start | bytes 230408 | tf_op jit(solution)/shard_map/ppermute | solution.py:25
  734.2 25.6 %collective-permute-start.28 = (f32[150,64,1]{0,1,2:T(8,128)S(1)}, f32[150,64,1]{0,1,2:T(8,128)S(1)}, u32[]{:S(2)}, u32[]{:S(2)}) collective-permute-start(f32[150,64,1]{0,1,2:T(8,128)S(1)} %copy.214), channel_id=1, source_target_pairs={{1,0},{2,1},{3,2},{4,3},{5,4},{6,5},{7,6},{0,7},{9,8},{10,9},{11,1... | collective-permute-start | bytes 115208 | tf_op jit(solution)/shard_map/ppermute | solution.py:25
  (57 other events, 673.7 us)
where the time goes:
time: 793 us; the launch traced here: 782 us
  local copies, waits for them, and re-layouts  322 us (41%)
  matrix products  128 us (16%)
  starting transfers between devices  121 us (15%)
  blocking collectives  110 us (14%)
  other arithmetic  91.2 us (12%)
  waiting for transfers between devices  8.03 us (1%)
    dot_general x8, matrix products, per_device(): jnp.einsum('ab,byx->ayx', blend_mat, current_ocean_snapshot, precision=high)  126 us
    all_gather x8, blocking collectives, per_device(): lax.all_gather(current_ocean_snapshot[:, row_count - 1, :], 'tx', axis=1,...  110 us
    unnamed x109, local copies, waits for them, and re-layouts  97.7 us
    slice x16, local copies, waits for them, and re-layouts, per_device(): current_ocean_snapshot[:, :, col_count - 1]  72.2 us
    slice x8, local copies, waits for them, and re-layouts, per_device(): jnp.roll(current_ocean_snapshot, 1, axis=2)  46.5 us
    ppermute x16, starting transfers between devices, with_halo(): lax.ppermute(tail, axis, [(i, (i + 1) % count) for i in range(ends)])  38.5 us
    ppermute x16, starting transfers between devices, with_halo(): lax.ppermute(head, axis, [((i + 1) % count, i) for i in range(ends)])  37.9 us
    slice x8, local copies, waits for them, and re-layouts, per_device(): current_ocean_snapshot[:, :, 0]  33.1 us
  transfers between devices with their start and end apart: 37, of which 2 were waited for; matrix products, arithmetic and copies ran while one was open for 33% of the time, Pallas kernels for 0%

commit v1 on v0

v1 whole, which is shorter than its diff:
```python
import functools

import jax
import jax.numpy as jnp
from jax import lax
from jax.experimental import pallas as pl
from jax.experimental.pallas import tpu as pltpu
from jax.sharding import PartitionSpec as P

NSTEP = 4
INTERVALS = 2
H = NSTEP
LANES = 128
CH = 150
CM = 152
CP = 160
MASK, FOLD, FORCE = 152, 153, 154

relaxation_speed = 0.3
flux_gain = 0.25
mix_gain = 0.1

PARAMS = pltpu.CompilerParams(vmem_limit_bytes=58 * 1024 * 1024)
VM = pl.BlockSpec(memory_space=pltpu.VMEM)
SM = pl.BlockSpec(memory_space=pltpu.SMEM)


def lane_ids(rows):
    return lax.broadcasted_iota(jnp.int32, (rows, LANES), 1)


def keep_edges(units, row, r, rows):
    unit = lax.rem(r // 16, 4)
    base = lax.rem(r, 16) * 8
    lane = lane_ids(rows)
    near = jnp.logical_and(lane >= base, lane < base + 8)
    pltpu.store(units.at[unit, pl.ds(0, rows)], pltpu.roll(row, base + 4, 1), mask=near)


def pack_strips(units, west_out, east_out):
    rows = west_out.shape[1]
    low = lax.rem(lane_ids(rows), 8) < 4
    for i in range(2):
        first, second = units[2 * i], units[2 * i + 1]
        west_out[i] = jnp.where(low, pltpu.roll(second, LANES - 4, 1), first)
        east_out[i] = jnp.where(low, first, pltpu.roll(second, 4, 1))


def turn_kernel(state_ref, rows_ref, west_ref, east_ref, units):
    count = rows_ref.shape[0]
    full = CH // 8 * 8

    def body(i, _):
        for k in range(4):
            y = i * 4 + k
            rows_ref[y, 0:full] = state_ref[pl.ds(y, full, stride=count), :]
            rows_ref[y, full:CH] = state_ref[pl.ds(full * count + y, CH - full, stride=count), :]
            rows_ref[y, CH:CM] = jnp.zeros((CM - CH, LANES), jnp.float32)
            keep_edges(units, rows_ref[y], y + H, CM)
        return 0

    lax.fori_loop(0, count // 4, body, 0)
    pack_strips(units, west_ref, east_ref)


def edge_kernel(rows_ref, west_ref, east_ref, units):
    count, rows = rows_ref.shape[0], rows_ref.shape[1]

    def body(i, _):
        for k in range(4):
            keep_edges(units, rows_ref[i * 4 + k], i * 4 + k + H, rows)
        return 0

    lax.fori_loop(0, count // 4, body, 0)
    pack_strips(units, west_ref, east_ref)


def split(x):
    high = x.astype(jnp.bfloat16)
    return high, (x - high.astype(jnp.float32)).astype(jnp.bfloat16)


def mix_pair(mix_ref, first, second):
    h0, l0 = split(first)
    h1, l1 = split(second)
    high = jnp.concatenate([h0, h1], axis=1)
    low = jnp.concatenate([l0, l1], axis=1)
    stack = jnp.concatenate([high, high, low], axis=0)
    return jnp.dot(mix_ref[...], stack, preferred_element_type=jnp.float32)


CHUNK = 40


def steps_kernel(
    last, info_ref, rows_hbm, pads_ref, west_ref, east_ref, north_ref, south_ref, top_hbm, mix_ref, diff_ref,
    out_ref, a_ref, b_ref, sa_ref, sb_ref, edge_ref, wa_ref, wb_ref, fold_ref, lhs_ref, sem,
):
    count = rows_hbm.shape[0]
    tiles = wa_ref.shape[0]
    is_fold = info_ref[0] == 1
    own = info_ref[1]
    copy = pltpu.make_async_copy(rows_hbm, a_ref.at[pl.ds(H, count), pl.ds(0, CM)], sem.at[0])
    copy.start()

    @pl.when(is_fold)
    def _():
        tops = pltpu.make_async_copy(top_hbm, wa_ref.at[:, pl.ds(0, H)], sem.at[1])
        tops.start()
        tops.wait()
        for j in range(tiles):
            source = wa_ref[j, H - 1, FOLD : FOLD + 1, :]
            for block in range(tiles):
                at = (lax.broadcasted_iota(jnp.int32, (LANES, LANES), 0) + block * LANES).astype(jnp.float32)
                hit = jnp.where(at == source, 1.0, 0.0).astype(jnp.bfloat16)
                fold_ref[block * LANES : (block + 1) * LANES, j * LANES : (j + 1) * LANES] = hit

    lane = lane_ids(CP)
    low = lax.rem(lane, 8) < 4
    for i in range(2):
        fw, fe = west_ref[i], east_ref[i]
        sa_ref[2 * i] = jnp.where(low, fw, fe)
        sa_ref[2 * i + 1] = jnp.where(low, pltpu.roll(fw, LANES - 4, 1), pltpu.roll(fe, 4, 1))
    wrapped = sa_ref[0]
    sa_ref[0] = jnp.where(lane < 8 * H, south_ref[H], wrapped)
    sa_ref[4] = jnp.where(lane < 8 * H, wrapped, jnp.where(lane < 16 * H, north_ref[H], 0.0))
    edge_ref[...] = jnp.zeros(edge_ref.shape, jnp.float32)
    for k in range(H):
        a_ref[k] = south_ref[k]
        a_ref[count + H + k] = north_ref[k]
    b_ref[0] = jnp.zeros((CP, LANES), jnp.float32)
    b_ref[count + 2 * H - 1] = jnp.zeros((CP, LANES), jnp.float32)

    def set_pads(y, _):
        a_ref[y + H, CM:CP] = pads_ref[y]
        return 0

    copy.wait()
    lax.fori_loop(0, count, set_pads, 0, unroll=8)

    part_lane = lane_ids(CHUNK)
    chunks = [(c, slice(c, c + CHUNK)) for c in range(0, CP, CHUNK)]

    def fold_part(step, src, strip, w_src, w_dst):
        for j in range(tiles):
            high, below = split(w_src[j, H - 1])
            lhs_ref[0:CP, j * LANES : (j + 1) * LANES] = high
            lhs_ref[CP : 2 * CP, j * LANES : (j + 1) * LANES] = below
        for p in range(tiles // 2):
            both = jnp.dot(
                lhs_ref[...], fold_ref[:, 2 * p * LANES : 2 * (p + 1) * LANES], preferred_element_type=jnp.float32
            )
            both = both[0:CP] + both[CP : 2 * CP]
            w_src[2 * p, H] = both[:, 0:LANES]
            w_src[2 * p + 1, H] = both[:, LANES : 2 * LANES]
        src[count + H] = w_src[own, H]
        before, after = w_src[lax.rem(own + tiles - 1, tiles), H], w_src[lax.rem(own + 1, tiles), H]
        base = 8 * ((count + H) % 16)
        beside = jnp.where(low, pltpu.roll(before, base + 4, 1), pltpu.roll(after, base + 4, 1))
        strip[4] = jnp.where(jnp.logical_and(lane >= base, lane < base + 8), beside, strip[4])
        if step == NSTEP - 1:
            return

        def pair(i, _):
            k = step + 1 + i // (tiles // 2)
            j = lax.rem(i, tiles // 2) * 2
            mixed = mix_pair(mix_ref, w_src[j, k], w_src[j + 1, k])
            for m in range(2):
                here = j + m
                mask = w_src[here, k, MASK : MASK + 1, :]
                left, right = lax.rem(here + tiles - 1, tiles), lax.rem(here + 1, tiles)
                for _, ch in chunks:
                    c = w_src[here, k, ch]
                    a = jnp.where(part_lane == LANES - 1, w_src[left, k, ch], c)
                    b = jnp.where(part_lane == 0, w_src[right, k, ch], c)
                    total = pltpu.roll(a, 1, 1) + pltpu.roll(b, LANES - 1, 1)
                    total = total + (w_src[here, k - 1, ch] + w_src[here, k + 1, ch])
                    change = diff_ref[ch] * total + mixed[ch, m * LANES : (m + 1) * LANES]
                    w_dst[here, k, ch] = c + mask * change
            return 0

        lax.fori_loop(0, (H - 1 - step) * (tiles // 2), pair, 0)

    def main_part(step, src, dst, strip):
        ends = step == NSTEP - 1
        unroll = 4 if ends else 5
        first = H if ends else 1

        def body(i, _):
            start = first + i * (2 * unroll)
            mixed = [mix_pair(mix_ref, src[start + 2 * p], src[start + 2 * p + 1]) for p in range(unroll)]
            for q in range(2 * unroll):
                r = start + q
                unit = r // 16
                base = lax.rem(r, 16) * 8
                mask = src[r, MASK : MASK + 1, :]
                near = jnp.logical_and(part_lane >= base, part_lane < base + 8)
                for c0, ch in chunks:
                    c = src[r, ch]
                    beside = pltpu.roll(strip[unit, ch], LANES - 4 - base, 1)
                    a = jnp.where(part_lane == LANES - 1, beside, c)
                    b = jnp.where(part_lane == 0, beside, c)
                    total = pltpu.roll(a, 1, 1) + pltpu.roll(b, LANES - 1, 1)
                    total = total + (src[r - 1, ch] + src[r + 1, ch])
                    change = diff_ref[ch] * total + mixed[q // 2][ch, (q % 2) * LANES : (q % 2 + 1) * LANES]
                    new = c + mask * change
                    if not ends:
                        dst[r, ch] = new
                        pltpu.store(edge_ref.at[unit, pl.ds(c0, CHUNK)], pltpu.roll(c, base + 4, 1), mask=near)
                    elif last:
                        size = min(CHUNK, CH - c0)
                        out_ref[pl.ds(c0 * count + r - H, size, stride=count), :] = new[0:size]
                    else:
                        size = min(CHUNK, CM - c0)
                        out_ref[r - H, c0 : c0 + size] = new[0:size]
            return 0

        lax.fori_loop(0, (count if ends else count + 2 * H - 2) // (2 * unroll), body, 0)

    def strip_part(strip, strip_new):
        for u0, u1 in ((0, 1), (2, 3), (4, 4)):
            mixed = mix_pair(mix_ref, strip[u0], strip[u1])
            for m, u in enumerate((u0, u1) if u0 != u1 else (u0,)):
                mask = strip[u, MASK : MASK + 1, :]
                above, under = min(u + 1, 4), max(u - 1, 0)
                place = lax.rem(part_lane, 8)
                for _, ch in chunks:
                    c = strip[u, ch]
                    edges = edge_ref[u, ch]
                    a = jnp.where(place == 4, edges, c)
                    b = jnp.where(place == 3, edges, c)
                    total = pltpu.roll(a, LANES - 1, 1) + pltpu.roll(b, 1, 1)
                    n = pltpu.roll(jnp.where(part_lane < 8, strip[above, ch], c), LANES - 8, 1)
                    s = pltpu.roll(jnp.where(part_lane >= LANES - 8, strip[under, ch], c), 8, 1)
                    change = diff_ref[ch] * (total + (n + s)) + mixed[ch, m * LANES : (m + 1) * LANES]
                    strip_new[u, ch] = c + mask * change

    for step in range(NSTEP):
        even = step % 2 == 0
        src, dst = (a_ref, b_ref) if even else (b_ref, a_ref)
        strip, strip_new = (sa_ref, sb_ref) if even else (sb_ref, sa_ref)
        w_src, w_dst = (wa_ref, wb_ref) if even else (wb_ref, wa_ref)
        pl.when(is_fold)(functools.partial(fold_part, step, src, strip, w_src, w_dst))
        main_part(step, src, dst, strip)
        if step < NSTEP - 1:
            strip_part(strip, strip_new)


def f32(*shape):
    return jax.ShapeDtypeStruct(shape, jnp.float32)


def shift(x, axis, by, closed):
    count = lax.axis_size(axis)
    pairs = [(i, (i + by) % count) for i in range(count) if closed or 0 <= i + by < count]
    return lax.ppermute(x, axis, pairs)


def per_device(state, diffusivity, mixing, ocean_mask, flux_dest, flux_target, flux_weight, fold_source):
    _, channels, row_count, col_count = state.shape
    levels = channels // 2
    tx_count = lax.axis_size("tx")
    is_ocean = lax.axis_index("comp") == 1
    northmost = lax.axis_index("ty") == lax.axis_size("ty") - 1
    tile_count = lax.axis_size("ty") * tx_count
    slots = max(2, 2 * row_count // tile_count)
    info = jnp.stack([jnp.logical_and(is_ocean, northmost).astype(jnp.int32), lax.axis_index("tx").astype(jnp.int32)])

    diffuse = diffusivity[0]
    service = jnp.where(is_ocean, flux_gain, relaxation_speed)
    own_surface = jnp.where(is_ocean, 0.0, relaxation_speed)
    ids = jnp.arange(channels)
    surface_row = jnp.logical_or(ids == 0, ids == levels)
    centre = 4.0 * diffuse + jnp.where(surface_row, own_surface, 0.0)
    matrix = mix_gain * mixing[0] - jnp.where(ids[:, None] == ids[None, :], centre[:, None], 0.0)
    matrix = jnp.pad(matrix, ((0, CP - channels), (0, CP - channels)))
    at_row = lax.broadcasted_iota(jnp.int32, (CP, CP), 0)
    at_col = lax.broadcasted_iota(jnp.int32, (CP, CP), 1)
    forced = jnp.logical_or(
        jnp.logical_and(at_row == 0, at_col == FORCE), jnp.logical_and(at_row == levels, at_col == FORCE + 1)
    )
    matrix = jnp.where(forced, service, matrix)
    high = lax.reduce_precision(matrix, 8, 7)
    rest = (matrix - high).astype(jnp.bfloat16)
    high = high.astype(jnp.bfloat16)
    mix = jnp.concatenate([high, rest, high], axis=1)
    diff = jnp.broadcast_to(jnp.pad(diffuse, (0, CP - channels))[:, None], (CP, LANES))

    dest_tile = flux_dest[0, :, 0]
    target = flux_target[0]
    tile_hit = (dest_tile[:, None] == jnp.arange(tile_count, dtype=jnp.int32)[None, :]).astype(jnp.int32)
    slot_rank = jnp.sum(tile_hit * (jnp.cumsum(tile_hit, axis=0) - 1), axis=1)
    picker = (dest_tile * slots + slot_rank)[None, :] == jnp.arange(tile_count * slots, dtype=jnp.int32)[:, None]
    out_ids = jnp.sum(jnp.where(picker, target[None, :] + 1, 0), axis=1) - 1
    in_ids = lax.all_to_all(out_ids.reshape(tile_count, slots), ("ty", "tx"), split_axis=0, concat_axis=0, tiled=True)
    place = (in_ids.reshape(-1)[None, :] == jnp.arange(row_count, dtype=jnp.int32)[:, None]).astype(jnp.float32)
    pick = picker.astype(jnp.float32)
    send_mat = jnp.where(is_ocean, pick * flux_weight[0][None, :], place.T)
    take_mat = jnp.where(is_ocean, place, pick.T)

    sea_mask = jnp.where(is_ocean, ocean_mask.astype(jnp.float32), 1.0)
    fold_rows = jnp.broadcast_to(fold_source.astype(jnp.float32)[None, :], sea_mask.shape)
    blank = jnp.zeros_like(sea_mask)
    best = lax.Precision.HIGHEST

    rows = None
    for interval in range(INTERVALS):
        if interval == 0:
            surface = jnp.concatenate([state[0, 0], state[0, levels]], axis=1)
            rows, west, east = pl.pallas_call(
                turn_kernel,
                out_shape=(f32(row_count, CM, LANES), f32(2, CM, LANES), f32(2, CM, LANES)),
                in_specs=[VM],
                out_specs=(VM, VM, VM),
                scratch_shapes=[pltpu.VMEM((4, CM, LANES), jnp.float32)],
                compiler_params=PARAMS,
                name="turn",
            )(state.reshape(channels * row_count, col_count))
        else:
            surface = jnp.concatenate([rows[:, 0], rows[:, levels]], axis=1)
            west, east = pl.pallas_call(
                edge_kernel,
                out_shape=(f32(2, CM, LANES), f32(2, CM, LANES)),
                in_specs=[VM],
                out_specs=(VM, VM),
                scratch_shapes=[pltpu.VMEM((4, CM, LANES), jnp.float32)],
                compiler_params=PARAMS,
                name="edges",
            )(rows)
        other = shift(surface, "comp", 1, True)
        outgoing = jnp.dot(send_mat, other, precision=best).reshape(tile_count, slots, 2 * col_count)
        arrived = lax.all_to_all(outgoing, ("ty", "tx"), split_axis=0, concat_axis=0, tiled=True)
        force = jnp.dot(take_mat, arrived.reshape(tile_count * slots, 2 * col_count), precision=best)
        pads = jnp.stack(
            [sea_mask, fold_rows, force[:, :col_count], force[:, col_count:], blank, blank, blank, blank], axis=1
        )
        pad_west, pad_east = pl.pallas_call(
            edge_kernel,
            out_shape=(f32(2, CP - CM, LANES), f32(2, CP - CM, LANES)),
            in_specs=[VM],
            out_specs=(VM, VM),
            scratch_shapes=[pltpu.VMEM((4, CP - CM, LANES), jnp.float32)],
            compiler_params=PARAMS,
            name="pad_edges",
        )(pads)
        bottom = jnp.concatenate([rows[:H], pads[:H]], axis=1)
        top = jnp.concatenate([rows[row_count - H :], pads[row_count - H :]], axis=1)
        tops = lax.all_gather(top, "tx", axis=0, tiled=False)
        from_east = shift(jnp.concatenate([west, pad_west], axis=1), "tx", -1, True)
        from_west = shift(jnp.concatenate([east, pad_east], axis=1), "tx", 1, True)
        low = lax.broadcasted_iota(jnp.int32, (CP, LANES), 1) % 8 < 4
        strip = jnp.where(low, from_west[0], from_east[0])[None]
        from_south = shift(jnp.concatenate([top, strip], axis=0), "ty", 1, False)
        from_north = shift(jnp.concatenate([bottom, strip], axis=0), "ty", -1, False)
        last = interval == INTERVALS - 1
        rows = pl.pallas_call(
            functools.partial(steps_kernel, last),
            out_shape=f32(channels * row_count, col_count) if last else f32(row_count, CM, LANES),
            in_specs=[SM, pl.BlockSpec(memory_space=pl.ANY), VM, VM, VM, VM, VM, pl.BlockSpec(memory_space=pl.ANY), VM, VM],
            out_specs=VM,
            scratch_shapes=[
                pltpu.VMEM((row_count + 2 * H, CP, LANES), jnp.float32),
                pltpu.VMEM((row_count + 2 * H, CP, LANES), jnp.float32),
                pltpu.VMEM((5, CP, LANES), jnp.float32),
                pltpu.VMEM((5, CP, LANES), jnp.float32),
                pltpu.VMEM((5, CP, LANES), jnp.float32),
                pltpu.VMEM((tx_count, H + 1, CP, LANES), jnp.float32),
                pltpu.VMEM((tx_count, H + 1, CP, LANES), jnp.float32),
                pltpu.VMEM((tx_count * LANES, tx_count * LANES), jnp.bfloat16),
                pltpu.VMEM((2 * CP, tx_count * LANES), jnp.bfloat16),
                pltpu.SemaphoreType.DMA((2,)),
            ],
            compiler_params=PARAMS,
            name="steps",
        )(info, rows, pads, from_west, from_east, from_north, from_south, tops, mix, diff)
    return rows.reshape(1, channels, row_count, col_count)


def solution(mesh):
    in_specs = (
        P("comp", None, "ty", "tx"),
        P("comp", None),
        P("comp", None, None),
        P("ty", "tx"),
        P("tx", "ty", None),
        P("tx", "ty"),
        P("tx", "ty"),
        P("tx"),
    )
    out_specs = P("comp", None, "ty", "tx")
    return jax.shard_map(per_device, mesh=mesh, in_specs=in_specs, out_specs=out_specs, check_vma=False)
```

time: 793 us -> 362 us (0.46)
  local copies, waits for them, and re-layouts: 322 us -> 9.28 us
  Pallas kernels: 0 us -> 202 us
  matrix products: 128 us -> 1.27 us
  blocking collectives: 110 us -> 0 us
  other arithmetic: 91.2 us -> 10.6 us
  starting transfers between devices: 121 us -> 55.1 us
  waiting for transfers between devices: 8.03 us -> 63 us
  between operations: 2.21 us -> 13.9 us
    pallas_call x0 -> x6, Pallas kernels: none -> 202 us  [the longest x2 181 us: per_device(): pl.pallas_call(functools.partial(steps_kernel, last), out_shape=f32(chann...]
    slice x66 -> x7, local copies, waits for them, and re-layouts: 191 us -> 3.36 us  [the longest x4 2.26 us: per_device(): top = jnp.concatenate([rows[row_count - H:], pads[row_count - H:]], axis=1)]
    dot_general x16 -> x4, matrix products: 128 us -> 1.27 us  [the longest x2 0.76 us: per_device(): jnp.dot(send_mat, other, precision=best)]
    all_gather x8 -> x0, blocking collectives: 110 us -> none  [per_device(): lax.all_gather(current_ocean_snapshot[:, row_count - 1, :], 'tx', axis=1,...]
    unnamed x109 -> x34, local copies, waits for them, and re-layouts: 97.7 us -> 0.8 us
    add x23 -> x2, other arithmetic: 84.9 us -> 0.68 us  [the longest x1 0.67 us: per_device(): dest_tile * slots + slot_rank]
    ppermute x32 -> x10, starting transfers between devices: 76.4 us -> 19.8 us  [shift(): return lax.ppermute(x, axis, pairs)]
    ppermute x32 -> x10, waiting for transfers between devices: 0.21 us -> 46.5 us  [shift(): return lax.ppermute(x, axis, pairs)]
  transfers between devices with their start and end apart: 37 -> 15, of which waited for: 2 -> 10; matrix products, arithmetic and copies ran while one was open for 33% -> 3% of each run, Pallas kernels for 0% -> 6%
where the time goes in v1:
time: 362 us; the launch traced here: 356 us
  Pallas kernels  202 us (56%)
  waiting for transfers between devices  63 us (17%)
  starting transfers between devices  55.1 us (15%)
  between operations  13.9 us (4%)
  other arithmetic  10.6 us (3%)
  local copies, waits for them, and re-layouts  9.28 us (3%)
    pallas_call x2, Pallas kernels, per_device(): pl.pallas_call(functools.partial(steps_kernel, last), out_shape=f32(chann...  181 us
    ppermute x10, waiting for transfers between devices, shift(): return lax.ppermute(x, axis, pairs)  46.5 us
    all_to_all x2, starting transfers between devices, per_device(): lax.all_to_all(outgoing, ('ty', 'tx'), split_axis=0, concat_axis=0, tiled...  23.7 us
    ppermute x10, starting transfers between devices, shift(): return lax.ppermute(x, axis, pairs)  19.8 us
    all_to_all x2, waiting for transfers between devices, per_device(): lax.all_to_all(outgoing, ('ty', 'tx'), split_axis=0, concat_axis=0, tiled...  16.5 us
    all_to_all x1, starting transfers between devices, per_device(): lax.all_to_all(out_ids.reshape(tile_count, slots), ('ty', 'tx'), split_ax...  11.6 us
    pallas_call x1, Pallas kernels, per_device(): pl.pallas_call(turn_kernel, out_shape=(f32(row_count, CM, LANES), f32(2,...  10.3 us
  transfers between devices with their start and end apart: 15, of which 10 were waited for; matrix products, arithmetic and copies ran while one was open for 3% of the time, Pallas kernels for 6%

profile of v1, /device:TPU:9, one launch (start us, length us, event | category | flops | bytes accessed | tf_op | source)
XLA Modules:
  0.0 355.6 jit_solution(10796588618522857344)
XLA Ops:
  10.5 11.6 %all-to-all-start = ((s32[64,1,2]{2,1,0:T(1,128)}), s32[64,1,2]{2,1,0:T(1,128)S(1)}, u32[]{:S(2)}, u32[]{:S(2)}) async-start(s32[64,1,2]{2,1,0:T(1,128)} %bitcast.6), calls=%async_computation | async-start | bytes 65536 | tf_op jit(solution)/shard_map/all_to_all | solution.py:295
  23.6 10.3 %turn.1 = (f32[64,152,128]{2,1,0:T(8,128)}, f32[2,152,128]{2,1,0:T(8,128)}, f32[2,152,128]{2,1,0:T(8,128)}) custom-call(f32[9600,128]{1,0:T(8,128)} %bitcast.32), custom_call_target="tpu_custom_call" | custom-call | tf_op jit(solution)/shard_map/turn/pallas_call | solution.py:310
  37.6 11.2 %all-to-all-start.1 = ((f32[64,2,256]{2,1,0:T(2,128)}), f32[64,2,256]{2,1,0:T(2,128)S(1)}, u32[]{:S(2)}, u32[]{:S(2)}) async-start(f32[64,2,256]{2,1,0:T(2,128)} %reshape.154), calls=%async_computation.1 | async-start | bytes 262144 | tf_op jit(solution)/shard_map/all_to_all | solution.py:332
  48.9 8.8 %all-to-all-done.1 = f32[64,2,256]{2,1,0:T(2,128)S(1)} async-done(((f32[64,2,256]{2,1,0:T(2,128)}), f32[64,2,256]{2,1,0:T(2,128)S(1)}, u32[]{:S(2)}, u32[]{:S(2)}) %all-to-all-start.1) | async-done | bytes 131104 | tf_op jit(solution)/shard_map/all_to_all | solution.py:332
  59.4 2.8 pad_edges.2
  64.1 1.4 collective-permute-start.1
  65.5 2.3 collective-permute-done.2.east_ref
  67.7 3.2 collective-permute-done.1.west_ref
  71.1 1.9 collective-permute-start.4
  73.0 5.8 %collective-permute-start.3 = (f32[5,160,128]{2,1,0:T(8,128)S(1)}, f32[5,160,128]{2,1,0:T(8,128)S(1)}, u32[]{:S(2)}, u32[]{:S(2)}) collective-permute-start(f32[5,160,128]{2,1,0:T(8,128)S(1)} %get-tuple-element.40), channel_id=1, source_target_pairs={{8,0},{16,8},{24,16},{32,24},{40,32},{48,40},{56,48},{9,1},{17,9},... | collective-permute-start | bytes 1228808 | tf_op jit(solution)/shard_map/ppermute | solution.py:256
  80.3 7.1 %collective-permute-done.4.south_ref = f32[5,160,128]{2,1,0:T(8,128)S(1)} collective-permute-done((f32[5,160,128]{2,1,0:T(8,128)S(1)}, f32[5,160,128]{2,1,0:T(8,128)S(1)}, u32[]{:S(2)}, u32[]{:S(2)}) %collective-permute-start.4) | collective-permute-done | bytes 409632 | tf_op jit(solution)/shard_map/ppermute | solution.py:256
  87.4 8.2 %collective-permute-done.3.north_ref = f32[5,160,128]{2,1,0:T(8,128)S(1)} collective-permute-done((f32[5,160,128]{2,1,0:T(8,128)S(1)}, f32[5,160,128]{2,1,0:T(8,128)S(1)}, u32[]{:S(2)}, u32[]{:S(2)}) %collective-permute-start.3) | collective-permute-done | bytes 409632 | tf_op jit(solution)/shard_map/ppermute | solution.py:256
  96.3 89.3 %steps.2.rows_ref.rows_hbm = f32[64,152,128]{2,1,0:T(8,128)} custom-call(s32[2]{0:T(128)} %pad_add_fusion.info_ref, f32[64,152,128]{2,1,0:T(8,128)} %get-tuple-element.14.rows_hbm, f32[64,8,128]{2,1,0:T(8,128)} %copy-done, f32[2,160,128]{2,1,0:T(8,128)} %copy-done.7, f32[2,160,128]{2,1,0:T(8,128)} %copy-done.6, f32[5,160,128]{2,1,0:T(8,128)} %copy-done.3, ...), custom_call_target="tpu_custom_call" | custom-call | tf_op jit(solution)/shard_map/steps/pallas_call | solution.py:356
  186.8 3.1 collective-permute-done.5
  191.0 12.4 %all-to-all-start.2 = ((f32[64,2,256]{2,1,0:T(2,128)}), f32[64,2,256]{2,1,0:T(2,128)S(1)}, u32[]{:S(2)}, u32[]{:S(2)}) async-start(f32[64,2,256]{2,1,0:T(2,128)} %reshape.156), calls=%async_computation.2 | async-start | bytes 262144 | tf_op jit(solution)/shard_map/all_to_all | solution.py:332
  204.6 7.7 %all-to-all-done.2 = f32[64,2,256]{2,1,0:T(2,128)S(1)} async-done(((f32[64,2,256]{2,1,0:T(2,128)}), f32[64,2,256]{2,1,0:T(2,128)S(1)}, u32[]{:S(2)}, u32[]{:S(2)}) %all-to-all-start.2) | async-done | bytes 131104 | tf_op jit(solution)/shard_map/all_to_all | solution.py:332
  213.8 5.6 %edges.1 = (f32[2,152,128]{2,1,0:T(8,128)}, f32[2,152,128]{2,1,0:T(8,128)}) custom-call(f32[64,152,128]{2,1,0:T(8,128)} %steps.2.rows_ref.rows_hbm), custom_call_target="tpu_custom_call" | custom-call | tf_op jit(solution)/shard_map/edges/pallas_call | solution.py:321
  219.5 2.9 pad_edges.3
  226.0 5.9 %collective-permute-done.7.east_ref = f32[2,160,128]{2,1,0:T(8,128)S(1)} collective-permute-done((f32[2,160,128]{2,1,0:T(8,128)S(1)}, f32[2,160,128]{2,1,0:T(8,128)S(1)}, u32[]{:S(2)}, u32[]{:S(2)}) %collective-permute-start.7) | collective-permute-done | bytes 163872 | tf_op jit(solution)/shard_map/ppermute | solution.py:256
  232.0 2.2 collective-permute-start.9
  234.1 5.5 %collective-permute-start.8 = (f32[5,160,128]{2,1,0:T(8,128)S(1)}, f32[5,160,128]{2,1,0:T(8,128)S(1)}, u32[]{:S(2)}, u32[]{:S(2)}) collective-permute-start(f32[5,160,128]{2,1,0:T(8,128)S(1)} %get-tuple-element.38), channel_id=1, source_target_pairs={{8,0},{16,8},{24,16},{32,24},{40,32},{48,40},{56,48},{9,1},{17,9},... | collective-permute-start | bytes 1228808 | tf_op jit(solution)/shard_map/ppermute | solution.py:256
  239.7 4.5 %collective-permute-done.9.south_ref = f32[5,160,128]{2,1,0:T(8,128)S(1)} collective-permute-done((f32[5,160,128]{2,1,0:T(8,128)S(1)}, f32[5,160,128]{2,1,0:T(8,128)S(1)}, u32[]{:S(2)}, u32[]{:S(2)}) %collective-permute-start.9) | collective-permute-done | bytes 409632 | tf_op jit(solution)/shard_map/ppermute | solution.py:256
  244.2 12.2 %collective-permute-done.8.north_ref = f32[5,160,128]{2,1,0:T(8,128)S(1)} collective-permute-done((f32[5,160,128]{2,1,0:T(8,128)S(1)}, f32[5,160,128]{2,1,0:T(8,128)S(1)}, u32[]{:S(2)}, u32[]{:S(2)}) %collective-permute-start.8) | collective-permute-done | bytes 409632 | tf_op jit(solution)/shard_map/ppermute | solution.py:256
  257.2 91.6 %steps.3 = f32[9600,128]{1,0:T(8,128)} custom-call(s32[2]{0:T(128)} %pad_add_fusion.info_ref, f32[64,152,128]{2,1,0:T(8,128)} %steps.2.rows_ref.rows_hbm, f32[64,8,128]{2,1,0:T(8,128)} %copy-done.1, f32[2,160,128]{2,1,0:T(8,128)} %copy-done.9, f32[2,160,128]{2,1,0:T(8,128)} %copy-done.8, f32[5,160,128]{2,1,0:T(8,128)} %copy-done.5, ...), custom_call_target="tpu_custom_call" | custom-call | tf_op jit(solution)/shard_map/steps/pallas_call | solution.py:356
  (104 shorter events, 24.3 us)
Async XLA Ops:
  6.5 28.5 %copy-start.16 = (s32[128]{0:T(128)S(1)}, s32[128]{0:T(128)}, u32[]{:S(2)}) copy-start(s32[128]{0:T(128)} %param.15) | copy-start | bytes 1540
  6.5 29.9 %copy-start.15 = (f32[1,64]{1,0:T(1,128)S(1)}, f32[1,64]{1,0:T(1,128)}, u32[]{:S(2)}) copy-start(f32[1,64]{1,0:T(1,128)} %param.14) | copy-start | bytes 772
  6.5 42.3 %copy-start.13 = (s32[64,128]{1,0:T(8,128)S(1)}, s32[64,128]{1,0:T(8,128)}, u32[]{:S(2)}) copy-start(s32[64,128]{1,0:T(8,128)} %param.11) | copy-start | bytes 98308
  6.5 52.8 %copy-start.14 = (f32[1,150]{1,0:T(1,128)S(1)}, f32[1,150]{1,0:T(1,128)}, u32[]{:S(2)}) copy-start(f32[1,150]{1,0:T(1,128)} %param.9) | copy-start | bytes 1804
  6.5 52.8 %copy-start.12 = (f32[1,150,150]{2,0,1:T(1,128)S(1)}, f32[1,150,150]{2,0,1:T(1,128)}, u32[]{:S(2)}) copy-start(f32[1,150,150]{2,0,1:T(1,128)} %param.10) | copy-start | bytes 270004
  10.5 24.6 %all-to-all-start = ((s32[64,1,2]{2,1,0:T(1,128)}), s32[64,1,2]{2,1,0:T(1,128)S(1)}, u32[]{:S(2)}, u32[]{:S(2)}) async-start(s32[64,1,2]{2,1,0:T(1,128)} %bitcast.6), calls=%async_computation | async-start | bytes 65536 | tf_op jit(solution)/shard_map/all_to_all | solution.py:295
  22.8 13.6 %collective-permute-start = (f32[64,256]{1,0:T(8,128)S(1)}, f32[64,256]{1,0:T(8,128)S(1)}, u32[]{:S(2)}, u32[]{:S(2)}) collective-permute-start(f32[64,256]{1,0:T(8,128)S(1)} %pad_maximum_fusion.11), channel_id=1, source_target_pairs={{0,64},{64,0},{1,65},{65,1},{2,66},{66,2},{3,67},{67,3},{4,68},{68... | collective-permute-start | bytes 196616 | tf_op jit(solution)/shard_map/ppermute | solution.py:256
  33.9 28.4 %copy-start.11 = (f32[2,152,128]{2,1,0:T(8,128)S(1)}, f32[2,152,128]{2,1,0:T(8,128)}, u32[]{:S(2)}) copy-start(f32[2,152,128]{2,1,0:T(8,128)} %get-tuple-element.17) | copy-start | bytes 466948
  33.9 29.5 %copy-start.10 = (f32[2,152,128]{2,1,0:T(8,128)S(1)}, f32[2,152,128]{2,1,0:T(8,128)}, u32[]{:S(2)}) copy-start(f32[2,152,128]{2,1,0:T(8,128)} %get-tuple-element.15) | copy-start | bytes 466948
  37.6 20.1 %all-to-all-start.1 = ((f32[64,2,256]{2,1,0:T(2,128)}), f32[64,2,256]{2,1,0:T(2,128)S(1)}, u32[]{:S(2)}, u32[]{:S(2)}) async-start(f32[64,2,256]{2,1,0:T(2,128)} %reshape.154), calls=%async_computation.1 | async-start | bytes 262144 | tf_op jit(solution)/shard_map/all_to_all | solution.py:332
  48.8 46.7 %all-gather.5.cloned.1.call-start = ((), (), s32[]{:S(2)}) async-start(), calls=%async_computation.3 | async-start | bytes 2949120 | tf_op jit(solution)/shard_map/all_gather | solution.py:348
  63.0 4.8 %collective-permute-start.2 = (f32[2,160,128]{2,1,0:T(8,128)S(1)}, f32[2,160,128]{2,1,0:T(8,128)S(1)}, u32[]{:S(2)}, u32[]{:S(2)}) collective-permute-start(f32[2,160,128]{2,1,0:T(8,128)S(1)} %pad_maximum_fusion.7), channel_id=1, source_target_pairs={{0,7},{1,0},{2,1},{3,2},{4,3},{5,4},{6,5},{7,6},{8,15},{9,8},{10,9... | collective-permute-start | bytes 491528 | tf_op jit(solution)/shard_map/ppermute | solution.py:256
  64.1 6.9 %collective-permute-start.1 = (f32[2,160,128]{2,1,0:T(8,128)S(1)}, f32[2,160,128]{2,1,0:T(8,128)S(1)}, u32[]{:S(2)}, u32[]{:S(2)}) collective-permute-start(f32[2,160,128]{2,1,0:T(8,128)S(1)} %pad_maximum_fusion.6), channel_id=1, source_target_pairs={{0,1},{1,2},{2,3},{3,4},{4,5},{5,6},{6,7},{7,0},{8,9},{9,10},{10,1... | collective-permute-start | bytes 491528 | tf_op jit(solution)/shard_map/ppermute | solution.py:256
  67.7 28.6 %copy-start.6 = (f32[2,160,128]{2,1,0:T(8,128)}, f32[2,160,128]{2,1,0:T(8,128)S(1)}, u32[]{:S(2)}) copy-start(f32[2,160,128]{2,1,0:T(8,128)S(1)} %collective-permute-done.2.east_ref) | copy-start | bytes 491524
  71.0 25.3 %copy-start.7 = (f32[2,160,128]{2,1,0:T(8,128)}, f32[2,160,128]{2,1,0:T(8,128)S(1)}, u32[]{:S(2)}) copy-start(f32[2,160,128]{2,1,0:T(8,128)S(1)} %collective-permute-done.1.west_ref) | copy-start | bytes 491524
  71.1 16.3 %collective-permute-start.4 = (f32[5,160,128]{2,1,0:T(8,128)S(1)}, f32[5,160,128]{2,1,0:T(8,128)S(1)}, u32[]{:S(2)}, u32[]{:S(2)}) collective-permute-start(f32[5,160,128]{2,1,0:T(8,128)S(1)} %get-tuple-element.39), channel_id=1, source_target_pairs={{0,8},{8,16},{16,24},{24,32},{32,40},{40,48},{48,56},{1,9},{9,17},... | collective-permute-start | bytes 1228808 | tf_op jit(solution)/shard_map/ppermute | solution.py:256
  73.0 22.5 %collective-permute-start.3 = (f32[5,160,128]{2,1,0:T(8,128)S(1)}, f32[5,160,128]{2,1,0:T(8,128)S(1)}, u32[]{:S(2)}, u32[]{:S(2)}) collective-permute-start(f32[5,160,128]{2,1,0:T(8,128)S(1)} %get-tuple-element.40), channel_id=1, source_target_pairs={{8,0},{16,8},{24,16},{32,24},{40,32},{48,40},{56,48},{9,1},{17,9},... | collective-permute-start | bytes 1228808 | tf_op jit(solution)/shard_map/ppermute | solution.py:256
  186.7 3.2 collective-permute-start.5
  191.0 21.3 %all-to-all-start.2 = ((f32[64,2,256]{2,1,0:T(2,128)}), f32[64,2,256]{2,1,0:T(2,128)S(1)}, u32[]{:S(2)}, u32[]{:S(2)}) async-start(f32[64,2,256]{2,1,0:T(2,128)} %reshape.156), calls=%async_computation.2 | async-start | bytes 262144 | tf_op jit(solution)/shard_map/all_to_all | solution.py:332
  203.5 53.0 %all-gather.7.cloned.1.call-start = ((), (), s32[]{:S(2)}) async-start(), calls=%async_computation.4 | async-start | bytes 2949120 | tf_op jit(solution)/shard_map/all_gather | solution.py:348
  223.3 8.6 %collective-permute-start.7 = (f32[2,160,128]{2,1,0:T(8,128)S(1)}, f32[2,160,128]{2,1,0:T(8,128)S(1)}, u32[]{:S(2)}, u32[]{:S(2)}) collective-permute-start(f32[2,160,128]{2,1,0:T(8,128)S(1)} %pad_maximum_fusion.10), channel_id=1, source_target_pairs={{0,7},{1,0},{2,1},{3,2},{4,3},{5,4},{6,5},{7,6},{8,15},{9,8},{10,9... | collective-permute-start | bytes 491528 | tf_op jit(solution)/shard_map/ppermute | solution.py:256
  224.6 7.2 %collective-permute-start.6 = (f32[2,160,128]{2,1,0:T(8,128)S(1)}, f32[2,160,128]{2,1,0:T(8,128)S(1)}, u32[]{:S(2)}, u32[]{:S(2)}) collective-permute-start(f32[2,160,128]{2,1,0:T(8,128)S(1)} %pad_maximum_fusion.9), channel_id=1, source_target_pairs={{0,1},{1,2},{2,3},{3,4},{4,5},{5,6},{6,7},{7,0},{8,9},{9,10},{10,1... | collective-permute-start | bytes 491528 | tf_op jit(solution)/shard_map/ppermute | solution.py:256
  232.0 12.2 %collective-permute-start.9 = (f32[5,160,128]{2,1,0:T(8,128)S(1)}, f32[5,160,128]{2,1,0:T(8,128)S(1)}, u32[]{:S(2)}, u32[]{:S(2)}) collective-permute-start(f32[5,160,128]{2,1,0:T(8,128)S(1)} %get-tuple-element.37), channel_id=1, source_target_pairs={{0,8},{8,16},{16,24},{24,32},{32,40},{40,48},{48,56},{1,9},{9,17},... | collective-permute-start | bytes 1228808 | tf_op jit(solution)/shard_map/ppermute | solution.py:256
  234.1 22.3 %collective-permute-start.8 = (f32[5,160,128]{2,1,0:T(8,128)S(1)}, f32[5,160,128]{2,1,0:T(8,128)S(1)}, u32[]{:S(2)}, u32[]{:S(2)}) collective-permute-start(f32[5,160,128]{2,1,0:T(8,128)S(1)} %get-tuple-element.38), channel_id=1, source_target_pairs={{8,0},{16,8},{24,16},{32,24},{40,32},{48,40},{56,48},{9,1},{17,9},... | collective-permute-start | bytes 1228808 | tf_op jit(solution)/shard_map/ppermute | solution.py:256
  (8 other events, 79.3 us)
Sparse Core Ops, SparseCore 0:
  59.4 23.6 all-gather.4
  214.0 24.6 all-gather.6
